TPU v7x, 32 devices: a whole 2x2x4 slice. The times are simulated.
32 devices in a mesh: dp: 2 (over core), blk: 4 (over y, x), head: 4 (over z).
Axes of the slice: x: 2, y: 2, z: 4, core: 2. Of those that a mesh axis runs over, the one named last changes fastest.
Arguments:
- queries: bfloat16 [2, 2048, 4096], P('dp', ('blk', 'head')), may hold values from -8 to 8
- keys: bfloat16 [2, 2048, 512], P('dp', ('blk', 'head')), may hold values from -8 to 8
- values: bfloat16 [2, 2048, 512], P('dp', ('blk', 'head')), may hold values from -6 to 6
- lengths: int32 [2, 48], P('dp'), may hold values from 1 to 128, 2048 in all within a row
Outputs:
- attended: bfloat16 [2, 2048, 4096], P('dp', ('blk', 'head'))
Inputs may be any that keep to these rules, and one draw needn't show every extreme that they name: `lengths`: each row sums to 2048; the longest document has exactly 128 positions.
All inputs are finite; a program needn't handle non-finite values.
Results may differ from a plain program's by a relative error of at most 0.0035.
Values may be sent and summed in bfloat16 or wider, within the bound.
A program may use at most 64 MiB of HBM per device.

v0:
```python
import jax
import jax.numpy as jnp
from jax import lax
from jax.sharding import PartitionSpec as P

HEAD_DIM = 128


def from_behind(value, axis, by):
    count = lax.axis_size(axis)
    pairs = [(i, i + by) for i in range(count) if 0 <= i + by < count]
    return lax.ppermute(value, axis, pairs)


def on_device(queries, keys, values, lengths):
    ends = jnp.cumsum(lengths[0])
    scale = 1.0 / jnp.sqrt(jnp.float32(HEAD_DIM))

    def doc_of(pos):
        return jnp.sum((pos[:, None] >= ends[None, :]).astype(jnp.int32), axis=1)

    own_keys = keys[0]
    own_values = values[0]
    rows_here = queries.shape[1]
    spread = lax.axis_size(("blk", "head"))
    doc_most = rows_here * spread // 16
    near = (doc_most - 1) // rows_here + 1
    q_rows = queries[0]
    place = lax.axis_index(("blk", "head"))
    block = q_rows.shape[0]
    kv_count = own_keys.shape[1] // HEAD_DIM
    group = q_rows.shape[1] // own_keys.shape[1]
    rows = jnp.arange(block, dtype=jnp.int32)
    q_pos = place * block + rows
    q_doc = doc_of(q_pos)
    query_four = q_rows.reshape(block, kv_count, group, HEAD_DIM)

    def mask_for(offset):
        k_pos = (place - offset) * block + rows
        return (
            (q_doc[:, None] == doc_of(k_pos)[None, :])
            & (k_pos[None, :] <= q_pos[:, None])
            & (k_pos[None, :] >= 0)
        )

    def attend(state, key_block, value_block, allowed):
        run_max, run_total, accum = state
        key_three = key_block.reshape(block, kv_count, HEAD_DIM)
        value_three = value_block.reshape(block, kv_count, HEAD_DIM)
        scores = (
            jnp.einsum("qhgd,khd->hgqk", query_four, key_three, preferred_element_type=jnp.float32)
            * scale
        )
        scores = jnp.where(allowed, scores, jnp.float32(-1e30))
        new_max = jnp.maximum(run_max, jnp.max(scores, axis=-1))
        correction = jnp.exp(run_max - new_max)
        expo = jnp.exp(scores - new_max[..., None])
        new_total = run_total * correction + jnp.sum(expo, axis=-1)
        added = jnp.einsum(
            "hgqk,khd->qhgd",
            expo.astype(jnp.bfloat16),
            value_three,
            preferred_element_type=jnp.float32,
        )
        new_accum = accum * jnp.transpose(correction, (2, 0, 1))[..., None] + added
        return (new_max, new_total, new_accum)

    state = (
        jnp.full((kv_count, group, block), -1e30, jnp.float32),
        jnp.zeros((kv_count, group, block), jnp.float32),
        jnp.zeros((block, kv_count, group, HEAD_DIM), jnp.float32),
    )
    state = attend(state, own_keys, own_values, mask_for(0))
    moved = (own_keys, own_values)
    for offset in range(1, near + 1):
        moved = from_behind((own_keys, own_values), ("blk", "head"), offset)
        visit_allowed = mask_for(offset)
        state = attend(state, moved[0], moved[1], visit_allowed)
    run_max, run_total, accum = state
    result = accum / jnp.transpose(run_total, (2, 0, 1))[..., None]
    result = result.reshape(block, q_rows.shape[1]).astype(jnp.bfloat16)
    return result[None]


def solution(mesh):
    return jax.shard_map(
        on_device,
        mesh=mesh,
        in_specs=(
            P("dp", ("blk", "head"), None),
            P("dp", ("blk", "head"), None),
            P("dp", ("blk", "head"), None),
            P("dp", None),
        ),
        out_specs=P("dp", ("blk", "head"), None),
        check_vma=False,
    )
```

profile of v0, /device:TPU:0, one launch (start us, length us, event | category | flops | bytes accessed | tf_op | source)
XLA Modules:
  0.0 24.6 jit_solution(3895552490617626293)
XLA Ops:
  0.0 1.7 %copy.30 = bf16[1,128,512]{1,2,0:T(8,128)(2,1)} copy(bf16[1,128,512]{2,1,0:T(8,128)(2,1)} %param.5) | data formatting | bytes 262144 | tf_op args[1]
  1.7 4.9 %collective-permute-start = (bf16[128,512]{0,1:T(8,128)(2,1)}, bf16[128,512]{0,1:T(8,128)(2,1)S(1)}, u32[]{:S(2)}, u32[]{:S(2)}) collective-permute-start(bf16[128,512]{0,1:T(8,128)(2,1)} %bitcast.8), channel_id=1, source_target_pairs={{0,1},{1,2},{2,3},{3,4},{4,5},{5,6},{6,7},{7,8},{8,9},{9,10},{10,1... | collective-permute-start | bytes 393224 | tf_op jit(solution)/shard_map/ppermute | solution.py:12
  6.6 4.1 %collective-permute-start.1 = (bf16[128,512]{1,0:T(8,128)(2,1)}, bf16[128,512]{1,0:T(8,128)(2,1)}, u32[]{:S(2)}, u32[]{:S(2)}) collective-permute-start(bf16[128,512]{1,0:T(8,128)(2,1)} %bitcast.71), channel_id=1, source_target_pairs={{0,1},{1,2},{2,3},{3,4},{4,5},{5,6},{6,7},{7,8},{8,9},{9,10},{10,1... | collective-permute-start | bytes 393224 | tf_op jit(solution)/shard_map/ppermute | solution.py:12
  10.7 0.9 %reshape_squeeze.9 = bf16[128,4,128]{2,1,0:T(4,128)(2,1)S(1)} reshape(bf16[1,128,512]{2,1,0:T(8,128)(2,1)} %param.5) | data formatting | bytes 262144 | tf_op jit(solution)/shard_map/reshape;squeeze | solution.py:48
  11.7 0.7 %copy.25 = s32[48,1]{1,0:T(8,128)S(1)} copy(s32[48,1]{0,1:T(1,128)} %bitcast.73) | data formatting | bytes 384 | tf_op jit(solution)/shard_map/reshape.67
  12.4 0.1 reduce-window.8
  12.5 0.1 reduce
  12.6 1.5 %copy.47 = bf16[16,8,32,128]{3,2,1,0:T(8,128)(2,1)S(1)} copy(bf16[16,8,32,128]{3,1,2,0:T(8,128)(2,1)} %bitcast.66) | data formatting | bytes 2097152
  14.1 0.0 copy-start.2
  14.1 0.1 convert_reduce_fusion
  14.2 0.8 %and_and_fusion = (pred[128,128]{0,1:T(8,128)(4,1)}, pred[128,128]{0,1:T(8,128)(4,1)S(1)}) fusion(s32[128]{0:T(128)S(1)} %get-tuple-element.19, s32[128]{0:T(128)S(1)} %get-tuple-element.6, s32[128]{0:T(128)S(1)} %get-tuple-element.18, s32[128]{0:T(128)S(1)} %get-tuple-element.5, pred[128]{0:T(512)(128)(4,1)S(1)} %get-tuple-element.20, ...), kind=kLoop, calls=%fused_computation.19 | loop fusion | flops 131072 | bytes 35072 | tf_op jit(solution)/shard_map/and | solution.py:41
  14.9 0.7 %fusion.22 = (f32[4,8,128]{2,1,0:T(8,128)S(1)}, f32[4,8,128,128]{2,3,1,0:T(8,128)S(1)}) fusion(bf16[128,4,8,128]{3,2,1,0:T(8,128)(2,1)S(1)} %bitcast.64, bf16[128,4,128,1]{2,1,0,3:T(4,128)(2,1)S(1)} %bitcast.68, pred[128,128]{0,1:T(8,128)(4,1)S(1)} %get-tuple-element.13), kind=kOutput, calls=%fused_computation.38 | convolution fusion | flops 135786496 | bytes 3309568 | tf_op jit(solution)/shard_map/qhgd,khd->hgqk/dot_general | solution.py:51
  15.6 0.0 copy-done.2
  15.7 0.1 copy.44
  15.8 0.0 collective-permute-done
  15.8 1.4 %fusion.21 = (f32[4,8,128]{2,1,0:T(8,128)S(1)}, f32[4,8,128,128]{2,3,1,0:T(8,128)S(1)}) fusion(bf16[128,4,128,1]{0,2,3,1:T(8,128)(2,1)S(1)} %bitcast.70, bf16[128,4,8,128]{3,2,1,0:T(8,128)(2,1)S(1)} %bitcast.65, pred[128,128]{0,1:T(8,128)(4,1)} %get-tuple-element.12), kind=kOutput, calls=%fused_computation.37 | convolution fusion | flops 135786496 | bytes 3309568 | tf_op jit(solution)/shard_map/qhgd,khd->hgqk/dot_general | solution.py:51
  17.2 0.3 %fusion.3 = f32[4,8,128]{2,1,0:T(8,128)S(1)} fusion(f32[4,8,128,128]{2,3,1,0:T(8,128)S(1)} %get-tuple-element.17, f32[4,8,128]{2,1,0:T(8,128)S(1)} %get-tuple-element.11), kind=kLoop, calls=%fused_computation.9 | loop fusion | flops 1044480 | bytes 2129920 | tf_op jit(solution)/shard_map/reduce_sum | solution.py:58
  17.5 1.8 %fusion.8 = f32[4,8,128,128]{2,3,1,0:T(8,128)} fusion(bf16[128,4,128,1]{0,2,3,1:T(8,128)(2,1)S(1)} %bitcast.69, f32[4,8,128,128]{2,3,1,0:T(8,128)S(1)} %get-tuple-element.17, f32[4,8,128]{2,1,0:T(8,128)S(1)} %get-tuple-element.11), kind=kOutput, calls=%fused_computation.13 | convolution fusion | flops 135266304 | bytes 4341760 | tf_op jit(solution)/shard_map/hgqk,khd->qhgd/dot_general | solution.py:59
  19.3 0.0 copy-done
  19.3 0.4 %fusion.5 = f32[4,8,128]{2,1,0:T(8,128)S(1)} fusion(f32[4,8,128,128]{2,3,1,0:T(8,128)S(1)} %get-tuple-element.15, f32[4,8,128]{2,1,0:T(8,128)S(1)} %get-tuple-element.10), kind=kLoop, calls=%fused_computation.11 | loop fusion | flops 1044480 | bytes 2129920 | tf_op jit(solution)/shard_map/reduce_sum | solution.py:58
  19.7 0.0 collective-permute-done.1
  19.7 1.2 %copy.33 = bf16[128,512]{0,1:T(8,128)(2,1)S(1)} copy(bf16[128,512]{1,0:T(8,128)(2,1)} %collective-permute-done.1) | data formatting | bytes 262144 | tf_op jit(solution)/shard_map/ppermute | solution.py:12
  21.0 2.3 %fusion.1 = bf16[128,4,8,128]{0,3,2,1:T(8,128)(2,1)S(1)} fusion(f32[4,8,128,128]{2,3,1,0:T(8,128)S(1)} %copy-done.1, bf16[128,4,128,1]{0,2,3,1:T(8,128)(2,1)S(1)} %bitcast.72, f32[4,8,128,128]{2,3,1,0:T(8,128)} %copy-done, f32[128,4,8]{0,2,1:T(8,128)S(1)} %get-tuple-element.7, f32[4,8,128]{2,1,0:T(8,128)S(1)} %get-tuple-element.10, ...), kind=kOutput, calls=%fused_computation.2 | convolution fusion | flops 137887744 | bytes 5439488 | tf_op jit(solution)/shard_map/hgqk,khd->qhgd/dot_general | solution.py:59
  23.3 1.3 %copy.35 = bf16[1,128,4096]{2,1,0:T(8,128)(2,1)} copy(bf16[1,128,4096]{1,2,0:T(8,128)(2,1)S(1)} %bitcast.67) | data formatting | bytes 2097152 | tf_op jit(solution)/shard_map/convert_element_type | solution.py:81
  (7 shorter events, 0.0 us)
Async XLA Ops:
  1.7 14.1 %collective-permute-start = (bf16[128,512]{0,1:T(8,128)(2,1)}, bf16[128,512]{0,1:T(8,128)(2,1)S(1)}, u32[]{:S(2)}, u32[]{:S(2)}) collective-permute-start(bf16[128,512]{0,1:T(8,128)(2,1)} %bitcast.8), channel_id=1, source_target_pairs={{0,1},{1,2},{2,3},{3,4},{4,5},{5,6},{6,7},{7,8},{8,9},{9,10},{10,1... | collective-permute-start | bytes 393224 | tf_op jit(solution)/shard_map/ppermute | solution.py:12
  6.6 13.1 %collective-permute-start.1 = (bf16[128,512]{1,0:T(8,128)(2,1)}, bf16[128,512]{1,0:T(8,128)(2,1)}, u32[]{:S(2)}, u32[]{:S(2)}) collective-permute-start(bf16[128,512]{1,0:T(8,128)(2,1)} %bitcast.71), channel_id=1, source_target_pairs={{0,1},{1,2},{2,3},{3,4},{4,5},{5,6},{6,7},{7,8},{8,9},{9,10},{10,1... | collective-permute-start | bytes 393224 | tf_op jit(solution)/shard_map/ppermute | solution.py:12
  14.1 1.6 %copy-start.2 = (bf16[1,128,512]{2,1,0:T(8,128)(2,1)S(1)}, bf16[1,128,512]{2,1,0:T(8,128)(2,1)}, u32[]{:S(2)}) copy-start(bf16[1,128,512]{2,1,0:T(8,128)(2,1)} %param.6) | copy-start | bytes 393220
  17.2 2.1 %copy-start = (f32[4,8,128,128]{2,3,1,0:T(8,128)}, f32[4,8,128,128]{2,3,1,0:T(8,128)S(1)}, u32[]{:S(2)}) copy-start(f32[4,8,128,128]{2,3,1,0:T(8,128)S(1)} %get-tuple-element.15) | copy-start | bytes 6291460
  19.3 1.7 %copy-start.1 = (f32[4,8,128,128]{2,3,1,0:T(8,128)S(1)}, f32[4,8,128,128]{2,3,1,0:T(8,128)}, u32[]{:S(2)}) copy-start(f32[4,8,128,128]{2,3,1,0:T(8,128)} %fusion.8) | copy-start | bytes 6291460
where the time goes:
time: 24.9 us; the launch traced here: 24.6 us
  starting transfers between devices  9.05 us (36%)
  local copies, waits for them, and re-layouts  7.45 us (30%)
  matrix products  6.13 us (25%)
  other arithmetic  1.81 us (7%)
    ppermute x2, starting transfers between devices, from_behind(): return lax.ppermute(value, axis, pairs)  9.05 us
    dot_general x2, matrix products, attend(): jnp.einsum('hgqk,khd->qhgd', expo.astype(jnp.bfloat16), value_three, pref...  4.06 us
    unnamed x8, local copies, waits for them, and re-layouts  3.13 us
    dot_general x2, matrix products, attend(): jnp.einsum('qhgd,khd->hgqk', query_four, key_three, preferred_element_typ...  2.07 us
    convert_element_type x1, local copies, waits for them, and re-layouts, on_device(): result = result.reshape(block, q_rows.shape[1]).astype(jnp.bfloat16)  1.31 us
    ppermute x1, local copies, waits for them, and re-layouts, from_behind(): return lax.ppermute(value, axis, pairs)  1.21 us
    another operation x1, local copies, waits for them, and re-layouts, attend(): key_three = key_block.reshape(block, kv_count, HEAD_DIM)  0.94 us
    and x1, other arithmetic, mask_for(): (q_doc[:, None] == doc_of(k_pos)[None, :]) & (k_pos[None, :] <= q_pos[:,...  0.76 us
  transfers between devices with their start and end apart: 2, of which 0 were waited for; matrix products, arithmetic and copies ran while one was open for 36% of the time, Pallas kernels for 0%

commit v1 on v0

v1 whole, which is shorter than its diff:
```python
import functools
import math

import jax
import jax.numpy as jnp
from jax import lax
from jax.experimental import pallas as pl
from jax.experimental.pallas import tpu as pltpu
from jax.sharding import PartitionSpec as P

HEAD_DIM = 128
MESH = pl.DeviceIdType.MESH
MASKED = -1e30


def kernel(
    sizes, len_ref, q_hbm, k_hbm, v_hbm, out_ref,
    q_buf, k_own, k_far, v_all, own_scores, weights,
    load_sem, send_sem, recv_sem,
):
    blks, heads, near, rows, kv_count, group = sizes
    spread = blks * heads
    place = lax.axis_index("blk") * heads + lax.axis_index("head")

    def at(index):
        index = lax.rem(index + spread, spread)
        return {"blk": lax.div(index, heads), "head": lax.rem(index, heads)}

    def cols(h):
        return pl.ds(h * HEAD_DIM, HEAD_DIM)

    barrier = pltpu.get_barrier_semaphore()
    for offset in range(1, near + 1):
        pl.semaphore_signal(barrier, inc=1, device_id=at(place - offset), device_id_type=MESH)

    load_k = pltpu.make_async_copy(k_hbm.at[0], k_own, load_sem.at[0])
    load_q = pltpu.make_async_copy(q_hbm.at[0], q_buf, load_sem.at[1])
    load_v = [
        pltpu.make_async_copy(
            v_hbm.at[0, :, cols(h)], v_all.at[h, pl.ds(0, rows), pl.ds(0, HEAD_DIM)], load_sem.at[2 + h]
        )
        for h in range(kv_count)
    ]
    pl.semaphore_wait(barrier, near)

    def remote(offset, what, h):
        if what == 0:
            src, dst = k_hbm.at[0, :, cols(h)], k_far.at[h, pl.ds((offset - 1) * rows, rows), :]
        else:
            src = v_hbm.at[0, :, cols(h)]
            dst = v_all.at[h, pl.ds(offset * rows, rows), pl.ds(0, HEAD_DIM)]
        return pltpu.make_async_remote_copy(
            src_ref=src,
            dst_ref=dst,
            send_sem=send_sem.at[offset - 1, what, h],
            recv_sem=recv_sem.at[offset - 1, what, h],
            device_id=at(place + offset),
            device_id_type=MESH,
        )

    copies = {
        (offset, what, h): remote(offset, what, h)
        for what in range(2)
        for h in range(kv_count)
        for offset in range(1, near + 1)
    }
    for copy in copies.values():
        copy.start()
    load_k.start()
    load_q.start()
    for copy in load_v:
        copy.start()

    docs = len_ref.shape[1]
    row = lax.broadcasted_iota(jnp.int32, (docs, docs), 0)
    col = lax.broadcasted_iota(jnp.int32, (docs, docs), 1)
    down = jnp.sum(jnp.where(row == col, len_ref[...], 0), axis=1, keepdims=True)
    ends = jnp.sum(jnp.where(row <= col, down, 0), axis=0, keepdims=True)
    q_pos = place * rows + lax.broadcasted_iota(jnp.int32, (rows, 1), 0)
    first = jnp.max(jnp.where(ends <= q_pos, ends, 0), axis=1, keepdims=True)
    lane = lax.broadcasted_iota(jnp.int32, (rows, rows), 1)
    own_pos = place * rows + lane
    own_bias = jnp.where((own_pos >= first) & (own_pos <= q_pos), 0.0, MASKED)
    far_bias = jnp.concatenate(
        [jnp.where(own_pos - offset * rows >= first, 0.0, MASKED) for offset in range(1, near + 1)], axis=1
    )

    v_all[:, :, HEAD_DIM:] = jnp.ones((kv_count, (near + 1) * rows, HEAD_DIM), v_all.dtype)

    def scores_of(j, keys):
        return lax.dot_general(
            q_buf[:, cols(j)], keys, (((1,), (1,)), ((), ())), preferred_element_type=jnp.float32
        )

    load_k.wait()
    load_q.wait()
    for j in range(kv_count * group):
        own_scores[j] = scores_of(j, k_own[:, cols(j // group)]) + own_bias

    change = math.log2(math.e) / math.sqrt(HEAD_DIM)
    for h in range(kv_count):
        for offset in range(1, near + 1):
            copies[offset, 0, h].wait_recv()
        for j in range(h * group, (h + 1) * group):
            own = own_scores[j]
            far = scores_of(j, k_far[h]) + far_bias
            top = jnp.maximum(jnp.max(own, axis=1, keepdims=True), jnp.max(far, axis=1, keepdims=True))
            weights[j, :, :rows] = jnp.exp2((own - top) * change).astype(weights.dtype)
            weights[j, :, rows:] = jnp.exp2((far - top) * change).astype(weights.dtype)

    for h in range(kv_count):
        load_v[h].wait()
        for offset in range(1, near + 1):
            copies[offset, 1, h].wait_recv()
        for j in range(h * group, (h + 1) * group):
            summed = jnp.dot(weights[j], v_all[h], preferred_element_type=jnp.float32)
            out_ref[0, :, cols(j)] = (summed[:, :HEAD_DIM] / summed[:, HEAD_DIM:]).astype(out_ref.dtype)

    for copy in copies.values():
        copy.wait_send()


def solution(mesh):
    blks, heads = mesh.shape["blk"], mesh.shape["head"]

    def on_device(queries, keys, values, lengths):
        rows = queries.shape[1]
        kv_count = keys.shape[2] // HEAD_DIM
        group = queries.shape[2] // keys.shape[2]
        doc_most = rows * blks * heads // 16
        near = (doc_most - 1) // rows + 1
        span = (near + 1) * rows
        work = 4 * rows * span * queries.shape[2]
        return pl.pallas_call(
            functools.partial(kernel, (blks, heads, near, rows, kv_count, group)),
            out_shape=jax.ShapeDtypeStruct(queries.shape, queries.dtype),
            in_specs=[pl.BlockSpec(memory_space=pltpu.VMEM)] + [pl.BlockSpec(memory_space=pltpu.HBM)] * 3,
            out_specs=pl.BlockSpec(memory_space=pltpu.VMEM),
            scratch_shapes=[
                pltpu.VMEM(queries.shape[1:], queries.dtype),
                pltpu.VMEM(keys.shape[1:], keys.dtype),
                pltpu.VMEM((kv_count, near * rows, HEAD_DIM), keys.dtype),
                pltpu.VMEM((kv_count, span, 2 * HEAD_DIM), values.dtype),
                pltpu.VMEM((kv_count * group, rows, rows), jnp.float32),
                pltpu.VMEM((kv_count * group, rows, span), jnp.bfloat16),
                pltpu.SemaphoreType.DMA((2 + kv_count,)),
                pltpu.SemaphoreType.DMA((near, 2, kv_count)),
                pltpu.SemaphoreType.DMA((near, 2, kv_count)),
            ],
            compiler_params=pltpu.CompilerParams(
                collective_id=0, has_side_effects=True, vmem_limit_bytes=40 * 2**20
            ),
            cost_estimate=pl.CostEstimate(
                flops=work, bytes_accessed=4 * queries.size, transcendentals=work // (4 * HEAD_DIM)
            ),
        )(lengths, queries, keys, values)

    return jax.shard_map(
        on_device,
        mesh=mesh,
        in_specs=(
            P("dp", ("blk", "head"), None),
            P("dp", ("blk", "head"), None),
            P("dp", ("blk", "head"), None),
            P("dp", None),
        ),
        out_specs=P("dp", ("blk", "head"), None),
        check_vma=False,
    )
```

time: 24.9 us -> 18.6 us (0.75)
  Pallas kernels: 0 us -> 13.8 us
  starting transfers between devices: 9.05 us -> 0 us
  matrix products: 6.13 us -> 0 us
  local copies, waits for them, and re-layouts: 7.45 us -> 4.66 us
  other arithmetic: 1.81 us -> 0 us
    pallas_call x0 -> x1, Pallas kernels: none -> 13.8 us  [on_device(): pl.pallas_call(functools.partial(kernel, (blks, heads, near, rows, kv_cou...]
    ppermute x2 -> x0, starting transfers between devices: 9.05 us -> none  [from_behind(): return lax.ppermute(value, axis, pairs)]
    dot_general x4 -> x0, matrix products: 6.13 us -> none  [the longest x2 4.06 us: attend(): jnp.einsum('hgqk,khd->qhgd', expo.astype(jnp.bfloat16), value_three, pref...]
    another operation x3 -> x0, local copies, waits for them, and re-layouts: 1.8 us -> none  [the longest x1 0.94 us: attend(): key_three = key_block.reshape(block, kv_count, HEAD_DIM)]
    unnamed x8 -> x9, local copies, waits for them, and re-layouts: 3.13 us -> 4.66 us
    convert_element_type x1 -> x0, local copies, waits for them, and re-layouts: 1.31 us -> none  [on_device(): result = result.reshape(block, q_rows.shape[1]).astype(jnp.bfloat16)]
    ppermute x1 -> x0, local copies, waits for them, and re-layouts: 1.21 us -> none  [from_behind(): return lax.ppermute(value, axis, pairs)]
    reduce_sum x3 -> x0, other arithmetic: 0.83 us -> none  [the longest x2 0.74 us: attend(): new_total = run_total * correction + jnp.sum(expo, axis=-1)]
  transfers between devices with their start and end apart: 2 -> 0, of which waited for: 0 -> 0; matrix products, arithmetic and copies ran while one was open for 36% -> 0% of each run, Pallas kernels for 0% -> 0%
where the time goes in v1:
time: 18.6 us; the launch traced here: 18.4 us
  Pallas kernels  13.8 us (74%)
  local copies, waits for them, and re-layouts  4.66 us (25%)
    pallas_call x1, Pallas kernels, on_device(): pl.pallas_call(functools.partial(kernel, (blks, heads, near, rows, kv_cou...  13.8 us
    unnamed x9, local copies, waits for them, and re-layouts  4.66 us

profile of v1, /device:TPU:0, one launch (start us, length us, event | category | flops | bytes accessed | tf_op | source)
XLA Modules:
  0.0 18.4 jit_solution(2784133751027539907)
XLA Ops:
  0.0 0.0 copy-start
  0.0 1.2 %copy-done = bf16[1,128,4096]{2,1,0:T(8,128)(2,1)S(1)} copy-done((bf16[1,128,4096]{2,1,0:T(8,128)(2,1)S(1)}, bf16[1,128,4096]{2,1,0:T(8,128)(2,1)}, u32[]{:S(2)}) %copy-start) | copy-done | bytes 1048600
  1.2 0.0 copy-start.1
  1.2 0.9 %copy-done.1 = bf16[1,128,512]{2,1,0:T(8,128)(2,1)S(1)} copy-done((bf16[1,128,512]{2,1,0:T(8,128)(2,1)S(1)}, bf16[1,128,512]{2,1,0:T(8,128)(2,1)}, u32[]{:S(2)}) %copy-start.1) | copy-done | bytes 131096
  2.1 0.0 copy-start.2
  2.1 0.9 %copy-done.2 = bf16[1,128,512]{2,1,0:T(8,128)(2,1)S(1)} copy-done((bf16[1,128,512]{2,1,0:T(8,128)(2,1)S(1)}, bf16[1,128,512]{2,1,0:T(8,128)(2,1)}, u32[]{:S(2)}) %copy-start.2) | copy-done | bytes 131096
  3.0 0.0 copy-start.3
  3.0 0.7 %copy-done.3 = s32[1,48]{1,0:T(1,128)S(1)} copy-done((s32[1,48]{1,0:T(1,128)S(1)}, s32[1,48]{1,0:T(1,128)}, u32[]{:S(2)}) %copy-start.3) | copy-done | bytes 216
  3.7 13.8 %shard_map.46 = bf16[1,128,4096]{2,1,0:T(8,128)(2,1)S(1)} custom-call(s32[1,48]{1,0:T(1,128)S(1)} %copy-done.3, bf16[1,128,4096]{2,1,0:T(8,128)(2,1)S(1)} %copy-done, bf16[1,128,512]{2,1,0:T(8,128)(2,1)S(1)} %copy-done.1, bf16[1,128,512]{2,1,0:T(8,128)(2,1)S(1)} %copy-done.2), custom_call_target="tpu_custom_call" | custom-call | flops 536870912 | bytes 2097152 | tf_op jit(solution)/shard_map/pallas_call | solution.py:134
  17.5 1.0 %copy.6 = bf16[1,128,4096]{2,1,0:T(8,128)(2,1)} copy(bf16[1,128,4096]{2,1,0:T(8,128)(2,1)S(1)} %shard_map.46) | data formatting | bytes 2097152
Async XLA Ops:
  0.0 1.2 %copy-start = (bf16[1,128,4096]{2,1,0:T(8,128)(2,1)S(1)}, bf16[1,128,4096]{2,1,0:T(8,128)(2,1)}, u32[]{:S(2)}) copy-start(bf16[1,128,4096]{2,1,0:T(8,128)(2,1)} %q_hbm.1) | copy-start | bytes 3145732
  1.2 0.9 %copy-start.1 = (bf16[1,128,512]{2,1,0:T(8,128)(2,1)S(1)}, bf16[1,128,512]{2,1,0:T(8,128)(2,1)}, u32[]{:S(2)}) copy-start(bf16[1,128,512]{2,1,0:T(8,128)(2,1)} %k_hbm.1) | copy-start | bytes 393220
  2.1 0.9 %copy-start.2 = (bf16[1,128,512]{2,1,0:T(8,128)(2,1)S(1)}, bf16[1,128,512]{2,1,0:T(8,128)(2,1)}, u32[]{:S(2)}) copy-start(bf16[1,128,512]{2,1,0:T(8,128)(2,1)} %v_hbm.1) | copy-start | bytes 393220
  3.0 0.7 %copy-start.3 = (s32[1,48]{1,0:T(1,128)S(1)}, s32[1,48]{1,0:T(1,128)}, u32[]{:S(2)}) copy-start(s32[1,48]{1,0:T(1,128)} %len_ref.1) | copy-start | bytes 580

commit v2 on v1

--- a/solution.py
+++ b/solution.py
@@ -14,16 +14,15 @@
 
 
 def kernel(
-    sizes, len_ref, q_hbm, k_hbm, v_hbm, out_ref,
-    q_buf, k_own, k_far, v_all, own_scores, weights,
-    load_sem, send_sem, recv_sem,
+    sizes, len_hbm, q_hbm, k_hbm, v_hbm, out_hbm,
+    len_ref, q_buf, k_own, k_far, v_all, own_scores, weights, out_buf,
+    load_sem, send_sem, recv_sem, out_sem,
 ):
     blks, heads, near, rows, kv_count, group = sizes
     spread = blks * heads
     place = lax.axis_index("blk") * heads + lax.axis_index("head")
 
     def at(index):
-        index = lax.rem(index + spread, spread)
         return {"blk": lax.div(index, heads), "head": lax.rem(index, heads)}
 
     def cols(h):
@@ -31,17 +30,29 @@
 
     barrier = pltpu.get_barrier_semaphore()
     for offset in range(1, near + 1):
-        pl.semaphore_signal(barrier, inc=1, device_id=at(place - offset), device_id_type=MESH)
+
+        @pl.when(place >= offset)
+        def _():
+            pl.semaphore_signal(barrier, inc=1, device_id=at(place - offset), device_id_type=MESH)
 
     load_k = pltpu.make_async_copy(k_hbm.at[0], k_own, load_sem.at[0])
     load_q = pltpu.make_async_copy(q_hbm.at[0], q_buf, load_sem.at[1])
+    load_len = pltpu.make_async_copy(len_hbm, len_ref, load_sem.at[2 + kv_count])
     load_v = [
         pltpu.make_async_copy(
             v_hbm.at[0, :, cols(h)], v_all.at[h, pl.ds(0, rows), pl.ds(0, HEAD_DIM)], load_sem.at[2 + h]
         )
         for h in range(kv_count)
     ]
-    pl.semaphore_wait(barrier, near)
+    load_len.start()
+    load_k.start()
+    load_q.start()
+    for copy in load_v:
+        copy.start()
+
+    @pl.when(place < spread - 1)
+    def _():
+        pl.semaphore_wait(barrier, jnp.minimum(spread - 1 - place, near))
 
     def remote(offset, what, h):
         if what == 0:
@@ -58,19 +69,29 @@
             device_id_type=MESH,
         )
 
-    copies = {
-        (offset, what, h): remote(offset, what, h)
-        for what in range(2)
-        for h in range(kv_count)
-        for offset in range(1, near + 1)
-    }
-    for copy in copies.values():
-        copy.start()
-    load_k.start()
-    load_q.start()
-    for copy in load_v:
-        copy.start()
-
+    pieces = [(what, h) for what in range(2) for h in range(kv_count)]
+    for offset in range(1, near + 1):
+
+        @pl.when(place + offset < spread)
+        def _():
+            for piece in pieces:
+                remote(offset, *piece).start()
+
+        @pl.when(place < offset)
+        def _():
+            k_far[:, (offset - 1) * rows : offset * rows, :] = jnp.zeros((kv_count, rows, HEAD_DIM), k_far.dtype)
+            v_all[:, offset * rows : (offset + 1) * rows, :HEAD_DIM] = jnp.zeros(
+                (kv_count, rows, HEAD_DIM), v_all.dtype
+            )
+
+    def arrived(what, h):
+        for offset in range(1, near + 1):
+
+            @pl.when(place >= offset)
+            def _():
+                remote(offset, what, h).wait_recv()
+
+    load_len.wait()
     docs = len_ref.shape[1]
     row = lax.broadcasted_iota(jnp.int32, (docs, docs), 0)
     col = lax.broadcasted_iota(jnp.int32, (docs, docs), 1)
@@ -87,6 +108,12 @@
 
     v_all[:, :, HEAD_DIM:] = jnp.ones((kv_count, (near + 1) * rows, HEAD_DIM), v_all.dtype)
 
+    half = group // 2
+
+    def store(i):
+        part = pl.ds(i * half * HEAD_DIM, half * HEAD_DIM)
+        return pltpu.make_async_copy(out_buf.at[:, part], out_hbm.at[0, :, part], out_sem.at[i])
+
     def scores_of(j, keys):
         return lax.dot_general(
             q_buf[:, cols(j)], keys, (((1,), (1,)), ((), ())), preferred_element_type=jnp.float32
@@ -99,8 +126,7 @@
 
     change = math.log2(math.e) / math.sqrt(HEAD_DIM)
     for h in range(kv_count):
-        for offset in range(1, near + 1):
-            copies[offset, 0, h].wait_recv()
+        arrived(0, h)
         for j in range(h * group, (h + 1) * group):
             own = own_scores[j]
             far = scores_of(j, k_far[h]) + far_bias
@@ -110,14 +136,22 @@
 
     for h in range(kv_count):
         load_v[h].wait()
-        for offset in range(1, near + 1):
-            copies[offset, 1, h].wait_recv()
+        arrived(1, h)
         for j in range(h * group, (h + 1) * group):
             summed = jnp.dot(weights[j], v_all[h], preferred_element_type=jnp.float32)
-            out_ref[0, :, cols(j)] = (summed[:, :HEAD_DIM] / summed[:, HEAD_DIM:]).astype(out_ref.dtype)
-
-    for copy in copies.values():
-        copy.wait_send()
+            out_buf[:, cols(j)] = (summed[:, :HEAD_DIM] / summed[:, HEAD_DIM:]).astype(out_buf.dtype)
+            if (j + 1) % half == 0:
+                store(j // half).start()
+
+    for offset in range(1, near + 1):
+
+        @pl.when(place + offset < spread)
+        def _():
+            for piece in pieces:
+                remote(offset, *piece).wait_send()
+
+    for i in range(2 * kv_count):
+        store(i).wait()
 
 
 def solution(mesh):
@@ -134,21 +168,24 @@
         return pl.pallas_call(
             functools.partial(kernel, (blks, heads, near, rows, kv_count, group)),
             out_shape=jax.ShapeDtypeStruct(queries.shape, queries.dtype),
-            in_specs=[pl.BlockSpec(memory_space=pltpu.VMEM)] + [pl.BlockSpec(memory_space=pltpu.HBM)] * 3,
-            out_specs=pl.BlockSpec(memory_space=pltpu.VMEM),
+            in_specs=[pl.BlockSpec(memory_space=pl.ANY)] * 4,
+            out_specs=pl.BlockSpec(memory_space=pl.ANY),
             scratch_shapes=[
+                pltpu.VMEM(lengths.shape, lengths.dtype),
                 pltpu.VMEM(queries.shape[1:], queries.dtype),
                 pltpu.VMEM(keys.shape[1:], keys.dtype),
                 pltpu.VMEM((kv_count, near * rows, HEAD_DIM), keys.dtype),
                 pltpu.VMEM((kv_count, span, 2 * HEAD_DIM), values.dtype),
                 pltpu.VMEM((kv_count * group, rows, rows), jnp.float32),
                 pltpu.VMEM((kv_count * group, rows, span), jnp.bfloat16),
-                pltpu.SemaphoreType.DMA((2 + kv_count,)),
+                pltpu.VMEM(queries.shape[1:], queries.dtype),
+                pltpu.SemaphoreType.DMA((3 + kv_count,)),
                 pltpu.SemaphoreType.DMA((near, 2, kv_count)),
                 pltpu.SemaphoreType.DMA((near, 2, kv_count)),
+                pltpu.SemaphoreType.DMA((2 * kv_count,)),
             ],
             compiler_params=pltpu.CompilerParams(
-                collective_id=0, has_side_effects=True, vmem_limit_bytes=40 * 2**20
+                collective_id=0, has_side_effects=True, vmem_limit_bytes=60 * 2**20
             ),
             cost_estimate=pl.CostEstimate(
                 flops=work, bytes_accessed=4 * queries.size, transcendentals=work // (4 * HEAD_DIM)

time: 18.6 us -> 15.6 us (0.84)
  the two profiles are of different devices: /device:TPU:0 before, /device:TPU:4 now
where the time goes in v2:
time: 15.6 us; the launch traced here: 15.4 us
  Pallas kernels  13.1 us (84%)
  local copies, waits for them, and re-layouts  2.29 us (15%)
    pallas_call x1, Pallas kernels, on_device(): pl.pallas_call(functools.partial(kernel, (blks, heads, near, rows, kv_cou...  13.1 us
    unnamed x1, local copies, waits for them, and re-layouts  2.29 us

profile of v2, /device:TPU:4, one launch (start us, length us, event | category | flops | bytes accessed | tf_op | source)
XLA Modules:
  0.0 15.4 jit_solution(17515044442565492614)
XLA Ops:
  0.0 13.1 %shard_map.46 = bf16[1,128,4096]{2,1,0:T(8,128)(2,1)} custom-call(s32[1,48]{1,0:T(1,128)} %len_hbm.1, bf16[1,128,4096]{2,1,0:T(8,128)(2,1)} %q_hbm.1, bf16[1,128,512]{2,1,0:T(8,128)(2,1)} %k_hbm.1, bf16[1,128,512]{2,1,0:T(8,128)(2,1)} %v_hbm.1), custom_call_target="tpu_custom_call" | custom-call | flops 536870912 | bytes 2097152 | tf_op jit(solution)/shard_map/pallas_call | solution.py:168
  13.1 2.3 %copy.6 = bf16[1,128,4096]{2,1,0:T(8,128)(2,1)} copy(bf16[1,128,4096]{2,1,0:T(8,128)(2,1)} %shard_map.46) | data formatting | bytes 2097152

commit v3 on v2

--- a/solution.py
+++ b/solution.py
@@ -14,10 +14,12 @@
 
 
 def kernel(
-    sizes, len_hbm, q_hbm, k_hbm, v_hbm, out_hbm,
-    len_ref, q_buf, k_own, k_far, v_all, own_scores, weights, out_buf,
+    sizes, len_hbm, q_hbm, k_hbm, v_hbm, *refs
+):
+    (
+    *out, len_ref, q_buf, k_own, k_far, v_all, own_scores, weights, out_buf,
     load_sem, send_sem, recv_sem, out_sem,
-):
+    ) = refs
     blks, heads, near, rows, kv_count, group = sizes
     spread = blks * heads
     place = lax.axis_index("blk") * heads + lax.axis_index("head")
@@ -112,7 +114,7 @@
 
     def store(i):
         part = pl.ds(i * half * HEAD_DIM, half * HEAD_DIM)
-        return pltpu.make_async_copy(out_buf.at[:, part], out_hbm.at[0, :, part], out_sem.at[i])
+        return pltpu.make_async_copy(out_buf.at[:, part], out[i], out_sem.at[i])
 
     def scores_of(j, keys):
         return lax.dot_general(
@@ -154,6 +156,18 @@
         store(i).wait()
 
 
+def hand_on(*refs):
+    *parts, out, sem = refs
+    width = parts[0].shape[1]
+    copies = [
+        pltpu.make_async_copy(part, out.at[0, :, pl.ds(i * width, width)], sem.at[i]) for i, part in enumerate(parts)
+    ]
+    for copy in copies:
+        copy.start()
+    for copy in copies:
+        copy.wait()
+
+
 def solution(mesh):
     blks, heads = mesh.shape["blk"], mesh.shape["head"]
 
@@ -165,11 +179,13 @@
         near = (doc_most - 1) // rows + 1
         span = (near + 1) * rows
         work = 4 * rows * span * queries.shape[2]
-        return pl.pallas_call(
+        pieces = 2 * kv_count
+        width = queries.shape[2] // pieces
+        parts = pl.pallas_call(
             functools.partial(kernel, (blks, heads, near, rows, kv_count, group)),
-            out_shape=jax.ShapeDtypeStruct(queries.shape, queries.dtype),
+            out_shape=[jax.ShapeDtypeStruct((rows, width), queries.dtype)] * pieces,
             in_specs=[pl.BlockSpec(memory_space=pl.ANY)] * 4,
-            out_specs=pl.BlockSpec(memory_space=pl.ANY),
+            out_specs=[pl.BlockSpec(memory_space=pl.ANY)] * pieces,
             scratch_shapes=[
                 pltpu.VMEM(lengths.shape, lengths.dtype),
                 pltpu.VMEM(queries.shape[1:], queries.dtype),
@@ -191,6 +207,14 @@
                 flops=work, bytes_accessed=4 * queries.size, transcendentals=work // (4 * HEAD_DIM)
             ),
         )(lengths, queries, keys, values)
+        return pl.pallas_call(
+            hand_on,
+            out_shape=jax.ShapeDtypeStruct(queries.shape, queries.dtype),
+            in_specs=[pl.BlockSpec(memory_space=pl.ANY)] * pieces,
+            out_specs=pl.BlockSpec(memory_space=pl.ANY),
+            scratch_shapes=[pltpu.SemaphoreType.DMA((pieces,))],
+            cost_estimate=pl.CostEstimate(flops=0, bytes_accessed=4 * queries.size, transcendentals=0),
+        )(*parts)
 
     return jax.shard_map(
         on_device,

time: 15.6 us -> 46.2 us (2.96)
  Pallas kernels: 13.1 us -> 46 us
  local copies, waits for them, and re-layouts: 2.29 us -> 0 us
    pallas_call x0 -> x1, Pallas kernels: none -> 32.9 us  [on_device(): pl.pallas_call(hand_on, out_shape=jax.ShapeDtypeStruct(queries.shape, que...]
    unnamed x1 -> x0, local copies, waits for them, and re-layouts: 2.29 us -> none
where the time goes in v3:
time: 46.2 us; the launch traced here: 46 us
  Pallas kernels  46 us (100%)
    pallas_call x1, Pallas kernels, on_device(): pl.pallas_call(hand_on, out_shape=jax.ShapeDtypeStruct(queries.shape, que...  32.9 us
    pallas_call x1, Pallas kernels, on_device(): pl.pallas_call(functools.partial(kernel, (blks, heads, near, rows, kv_cou...  13.1 us

profile of v3, /device:TPU:4, one launch (start us, length us, event | category | flops | bytes accessed | tf_op | source)
XLA Modules:
  0.0 46.0 jit_solution(2575091204563340773)
XLA Ops:
  0.0 13.1 %shard_map.46 = (bf16[128,512]{1,0:T(8,128)(2,1)}, bf16[128,512]{1,0:T(8,128)(2,1)}, bf16[128,512]{1,0:T(8,128)(2,1)}, bf16[128,512]{1,0:T(8,128)(2,1)}, bf16[12...) custom-call(s32[1,48]{1,0:T(1,128)} %len_hbm.1, ...), custom_call_target="tpu_custom_call" | custom-call | flops 536870912 | bytes 2097152 | tf_op jit(solution)/shard_map/pallas_call | solution.py:184
  13.1 32.9 %shard_map.47 = bf16[1,128,4096]{2,1,0:T(8,128)(2,1)} custom-call(bf16[128,512]{1,0:T(8,128)(2,1)} %get-tuple-element.13.refs_0_, bf16[128,512]{1,0:T(8,128)(2,1)} %get-tuple-element.14.refs_1_, bf16[128,512]{1,0:T(8,128)(2,1)} %get-tuple-element.15.refs_2_, bf16[128,512]{1,0:T(8,128)(2,1)} %get-tuple-element.16.refs_3_, ...), custom_call_target="tpu_custom_call" | custom-call | bytes 2097152 | tf_op jit(solution)/shard_map/pallas_call | solution.py:210

commit v4 on v3

--- a/solution.py
+++ b/solution.py
@@ -17,8 +17,8 @@
     sizes, len_hbm, q_hbm, k_hbm, v_hbm, *refs
 ):
     (
-    *out, len_ref, q_buf, k_own, k_far, v_all, own_scores, weights, out_buf,
-    load_sem, send_sem, recv_sem, out_sem,
+    *out, len_ref, q_buf, k_own, k_far, v_all, own_scores, weights,
+    load_sem, send_sem, recv_sem,
     ) = refs
     blks, heads, near, rows, kv_count, group = sizes
     spread = blks * heads
@@ -112,10 +112,6 @@
 
     half = group // 2
 
-    def store(i):
-        part = pl.ds(i * half * HEAD_DIM, half * HEAD_DIM)
-        return pltpu.make_async_copy(out_buf.at[:, part], out[i], out_sem.at[i])
-
     def scores_of(j, keys):
         return lax.dot_general(
             q_buf[:, cols(j)], keys, (((1,), (1,)), ((), ())), preferred_element_type=jnp.float32
@@ -141,9 +137,7 @@
         arrived(1, h)
         for j in range(h * group, (h + 1) * group):
             summed = jnp.dot(weights[j], v_all[h], preferred_element_type=jnp.float32)
-            out_buf[:, cols(j)] = (summed[:, :HEAD_DIM] / summed[:, HEAD_DIM:]).astype(out_buf.dtype)
-            if (j + 1) % half == 0:
-                store(j // half).start()
+            out[j // half][:, cols(j % half)] = (summed[:, :HEAD_DIM] / summed[:, HEAD_DIM:]).astype(out[0].dtype)
 
     for offset in range(1, near + 1):
 
@@ -151,9 +145,6 @@
         def _():
             for piece in pieces:
                 remote(offset, *piece).wait_send()
-
-    for i in range(2 * kv_count):
-        store(i).wait()
 
 
 def hand_on(*refs):
@@ -185,7 +176,7 @@
             functools.partial(kernel, (blks, heads, near, rows, kv_count, group)),
             out_shape=[jax.ShapeDtypeStruct((rows, width), queries.dtype)] * pieces,
             in_specs=[pl.BlockSpec(memory_space=pl.ANY)] * 4,
-            out_specs=[pl.BlockSpec(memory_space=pl.ANY)] * pieces,
+            out_specs=[pl.BlockSpec(memory_space=pltpu.VMEM)] * pieces,
             scratch_shapes=[
                 pltpu.VMEM(lengths.shape, lengths.dtype),
                 pltpu.VMEM(queries.shape[1:], queries.dtype),
@@ -194,14 +185,12 @@
                 pltpu.VMEM((kv_count, span, 2 * HEAD_DIM), values.dtype),
                 pltpu.VMEM((kv_count * group, rows, rows), jnp.float32),
                 pltpu.VMEM((kv_count * group, rows, span), jnp.bfloat16),
-                pltpu.VMEM(queries.shape[1:], queries.dtype),
                 pltpu.SemaphoreType.DMA((3 + kv_count,)),
                 pltpu.SemaphoreType.DMA((near, 2, kv_count)),
                 pltpu.SemaphoreType.DMA((near, 2, kv_count)),
-                pltpu.SemaphoreType.DMA((2 * kv_count,)),
             ],
             compiler_params=pltpu.CompilerParams(
-                collective_id=0, has_side_effects=True, vmem_limit_bytes=60 * 2**20
+                collective_id=0, has_side_effects=True, vmem_limit_bytes=55440000
             ),
             cost_estimate=pl.CostEstimate(
                 flops=work, bytes_accessed=4 * queries.size, transcendentals=work // (4 * HEAD_DIM)
@@ -210,9 +199,10 @@
         return pl.pallas_call(
             hand_on,
             out_shape=jax.ShapeDtypeStruct(queries.shape, queries.dtype),
-            in_specs=[pl.BlockSpec(memory_space=pl.ANY)] * pieces,
+            in_specs=[pl.BlockSpec(memory_space=pltpu.VMEM)] * pieces,
             out_specs=pl.BlockSpec(memory_space=pl.ANY),
             scratch_shapes=[pltpu.SemaphoreType.DMA((pieces,))],
+            compiler_params=pltpu.CompilerParams(has_side_effects=False, vmem_limit_bytes=4 * 2**20),
             cost_estimate=pl.CostEstimate(flops=0, bytes_accessed=4 * queries.size, transcendentals=0),
         )(*parts)
 

time: 46.2 us -> 14.2 us (0.31)
  Pallas kernels: 46 us -> 13.4 us
  local copies, waits for them, and re-layouts: 0 us -> 0.65 us
    pallas_call x1, Pallas kernels: 32.9 us -> 1.03 us  [on_device(): pl.pallas_call(hand_on, out_shape=jax.ShapeDtypeStruct(queries.shape, que...]
    pallas_call x1, Pallas kernels: 13.1 us -> 12.4 us  [on_device(): pl.pallas_call(functools.partial(kernel, (blks, heads, near, rows, kv_cou...]
    unnamed x0 -> x2, local copies, waits for them, and re-layouts: none -> 0.65 us
where the time goes in v4:
time: 14.2 us; the launch traced here: 14.1 us
  Pallas kernels  13.4 us (94%)
  local copies, waits for them, and re-layouts  0.65 us (5%)
    pallas_call x1, Pallas kernels, on_device(): pl.pallas_call(functools.partial(kernel, (blks, heads, near, rows, kv_cou...  12.4 us
    pallas_call x1, Pallas kernels, on_device(): pl.pallas_call(hand_on, out_shape=jax.ShapeDtypeStruct(queries.shape, que...  1.03 us
    unnamed x2, local copies, waits for them, and re-layouts  0.65 us

profile of v4, /device:TPU:4, one launch (start us, length us, event | category | flops | bytes accessed | tf_op | source)
XLA Modules:
  0.0 14.1 jit_solution(12355012542076885272)
XLA Ops:
  0.0 0.0 copy-start
  0.0 0.7 %copy-done = s32[1,48]{1,0:T(1,128)S(1)} copy-done((s32[1,48]{1,0:T(1,128)S(1)}, s32[1,48]{1,0:T(1,128)}, u32[]{:S(2)}) %copy-start) | copy-done | bytes 216
  0.7 12.4 %shard_map.46 = (bf16[128,512]{1,0:T(8,128)(2,1)S(1)}, bf16[128,512]{1,0:T(8,128)(2,1)S(1)}, bf16[128,512]{1,0:T(8,128)(2,1)S(1)}, bf16[128,512]{1,0:T(8,128)(2,...) custom-call(s32[1,48]{1,0:T(1,128)S(1)} %copy-done, ...), custom_call_target="tpu_custom_call" | custom-call | flops 536870912 | bytes 2097152 | tf_op jit(solution)/shard_map/pallas_call | solution.py:175
  13.1 1.0 %shard_map.47 = bf16[1,128,4096]{2,1,0:T(8,128)(2,1)} custom-call(bf16[128,512]{1,0:T(8,128)(2,1)S(1)} %get-tuple-element.13.refs_0_, bf16[128,512]{1,0:T(8,128)(2,1)S(1)} %get-tuple-element.14.refs_1_, bf16[128,512]{1,0:T(8,128)(2,1)S(1)} %get-tuple-element.15.refs_2_, bf16[128,512]{1,0:T(8,128)(2,1)S(1)} %get-tuple-element.16.refs_3_, ...), custom_call_target="tpu_custom_call" | custom-call | bytes 2097152 | tf_op jit(solution)/shard_map/pallas_call | solution.py:199
Async XLA Ops:
  0.0 0.7 %copy-start = (s32[1,48]{1,0:T(1,128)S(1)}, s32[1,48]{1,0:T(1,128)}, u32[]{:S(2)}) copy-start(s32[1,48]{1,0:T(1,128)} %len_hbm.1) | copy-start | bytes 580

commit v5 on v4

--- a/solution.py
+++ b/solution.py
@@ -150,8 +150,15 @@
 def hand_on(*refs):
     *parts, out, sem = refs
     width = parts[0].shape[1]
+    half = parts[0].shape[0] // 2
     copies = [
-        pltpu.make_async_copy(part, out.at[0, :, pl.ds(i * width, width)], sem.at[i]) for i, part in enumerate(parts)
+        pltpu.make_async_copy(
+            part.at[pl.ds(r * half, half), :],
+            out.at[0, pl.ds(r * half, half), pl.ds(i * width, width)],
+            sem.at[2 * i + r],
+        )
+        for i, part in enumerate(parts)
+        for r in range(2)
     ]
     for copy in copies:
         copy.start()
@@ -201,7 +208,7 @@
             out_shape=jax.ShapeDtypeStruct(queries.shape, queries.dtype),
             in_specs=[pl.BlockSpec(memory_space=pltpu.VMEM)] * pieces,
             out_specs=pl.BlockSpec(memory_space=pl.ANY),
-            scratch_shapes=[pltpu.SemaphoreType.DMA((pieces,))],
+            scratch_shapes=[pltpu.SemaphoreType.DMA((2 * pieces,))],
             compiler_params=pltpu.CompilerParams(has_side_effects=False, vmem_limit_bytes=4 * 2**20),
             cost_estimate=pl.CostEstimate(flops=0, bytes_accessed=4 * queries.size, transcendentals=0),
         )(*parts)

time: 14.2 us -> 14.3 us (level)
  no operation moved by 1% of the time
where the time goes in v5:
time: 14.3 us; the launch traced here: 14.1 us
  Pallas kernels  13.5 us (94%)
  local copies, waits for them, and re-layouts  0.65 us (5%)
    pallas_call x1, Pallas kernels, on_device(): pl.pallas_call(functools.partial(kernel, (blks, heads, near, rows, kv_cou...  12.4 us
    pallas_call x1, Pallas kernels, on_device(): pl.pallas_call(hand_on, out_shape=jax.ShapeDtypeStruct(queries.shape, que...  1.09 us
    unnamed x2, local copies, waits for them, and re-layouts  0.65 us

profile of v5, /device:TPU:4, one launch (start us, length us, event | category | flops | bytes accessed | tf_op | source)
XLA Modules:
  0.0 14.1 jit_solution(11179685345616901925)
XLA Ops:
  0.0 0.0 copy-start
  0.0 0.7 %copy-done = s32[1,48]{1,0:T(1,128)S(1)} copy-done((s32[1,48]{1,0:T(1,128)S(1)}, s32[1,48]{1,0:T(1,128)}, u32[]{:S(2)}) %copy-start) | copy-done | bytes 216
  0.7 12.4 %shard_map.46 = (bf16[128,512]{1,0:T(8,128)(2,1)S(1)}, bf16[128,512]{1,0:T(8,128)(2,1)S(1)}, bf16[128,512]{1,0:T(8,128)(2,1)S(1)}, bf16[128,512]{1,0:T(8,128)(2,...) custom-call(s32[1,48]{1,0:T(1,128)S(1)} %copy-done, ...), custom_call_target="tpu_custom_call" | custom-call | flops 536870912 | bytes 2097152 | tf_op jit(solution)/shard_map/pallas_call | solution.py:182
  13.1 1.1 %shard_map.47 = bf16[1,128,4096]{2,1,0:T(8,128)(2,1)} custom-call(bf16[128,512]{1,0:T(8,128)(2,1)S(1)} %get-tuple-element.13.refs_0_, bf16[128,512]{1,0:T(8,128)(2,1)S(1)} %get-tuple-element.14.refs_1_, bf16[128,512]{1,0:T(8,128)(2,1)S(1)} %get-tuple-element.15.refs_2_, bf16[128,512]{1,0:T(8,128)(2,1)S(1)} %get-tuple-element.16.refs_3_, ...), custom_call_target="tpu_custom_call" | custom-call | bytes 2097152 | tf_op jit(solution)/shard_map/pallas_call | solution.py:206
Async XLA Ops:
  0.0 0.7 %copy-start = (s32[1,48]{1,0:T(1,128)S(1)}, s32[1,48]{1,0:T(1,128)}, u32[]{:S(2)}) copy-start(s32[1,48]{1,0:T(1,128)} %len_hbm.1) | copy-start | bytes 580
